TPU v7x, 128 devices: a whole 4x4x4 slice. The times are simulated.
128 devices in a mesh: pop: 4 (over y_hi, core), tp: 16 (over z, x), pp: 2 (over y_lo).
Axes of the slice: x: 4, y: 4 (y_hi: 2, y_lo: 2; y = y_hi * 2 + y_lo), z: 4, core: 2. Of those that a mesh axis runs over, the one named last changes fastest.
Arguments:
- hidden_in: bfloat16 [256, 8, 4096], P('tp', 'pop'), may hold values from -6 to 6
- norm_gain: float32 [2, 4096], P('pp'), may hold values from 0.5 to 1.5
- w_gate: bfloat16 [2, 4096, 12288], P('pp', None, 'tp'), may hold values from -0.09375 to 0.09375
- w_up: bfloat16 [2, 4096, 12288], P('pp', None, 'tp'), may hold values from -0.09375 to 0.09375
- w_down: bfloat16 [2, 12288, 4096], P('pp', 'tp'), may hold values from -0.0546875 to 0.0546875
- gate_left: bfloat16 [2, 8, 4096], P('pp', 'pop'), may hold values from -6 to 6
- gate_right: bfloat16 [2, 8, 12288], P('pp', 'pop', 'tp'), may hold values from -6 to 6
- up_left: bfloat16 [2, 8, 4096], P('pp', 'pop'), may hold values from -6 to 6
- up_right: bfloat16 [2, 8, 12288], P('pp', 'pop', 'tp'), may hold values from -6 to 6
- down_left: bfloat16 [2, 8, 12288], P('pp', 'pop', 'tp'), may hold values from -6 to 6
- down_right: bfloat16 [2, 8, 4096], P('pp', 'pop'), may hold values from -6 to 6
- ranks: int32 [8], P('pop'), may hold values from 0 to 7, each once
Outputs:
- section_out: bfloat16 [2, 256, 8, 4096], P('pp', 'tp', 'pop')
- update_gate: bfloat16 [2, 4096, 12288], P('pp', 'pop', 'tp')
- update_up: bfloat16 [2, 4096, 12288], P('pp', 'pop', 'tp')
- update_down: bfloat16 [2, 12288, 4096], P('pp', 'tp', 'pop')
Inputs may be any that keep to these rules, and one draw needn't show every extreme that they name: `ranks`: each number from 0 to 7 is the rank of exactly one member.
All inputs are finite; a program needn't handle non-finite values.
Results may differ from a plain program's by a relative error of at most 0.014.
Values may be sent and summed in bfloat16 or wider, within the bound.
No kernel may reach another device: no remote copies, remote signals or barrier semaphores. Data moves between devices by JAX's collectives and lax.ppermute only.
A program may use at most 128 MiB of HBM per device.

v0:
```python
import math
import jax
import jax.numpy as jnp
from jax import lax
from jax.sharding import PartitionSpec as P

sigma_scale = 0.3
norm_eps = 1e-05


def from_behind(block, axis, distance):
    devices = range(lax.axis_size(axis))
    route = [(i - distance, i) for i in devices if i - distance in devices]
    return lax.ppermute(block, axis, route)


def sent_together(arrays, axis, dim, along):
    both = jnp.concatenate(arrays, axis=along)
    out, at, done = (lax.all_gather(both, axis, axis=dim, tiled=True), 0, [])
    for a in arrays:
        done.append(lax.slice_in_dim(out, at, at + a.shape[along], axis=along))
        at += a.shape[along]
    return tuple(done)


def feed_forward(
    block,
    gain,
    w_gate,
    w_up,
    w_down,
    gate_left,
    gate_right,
    up_left,
    up_right,
    down_left,
    down_right,
):
    values = block.astype(jnp.float32)
    mean_sq = jnp.mean(values * values, axis=-1, keepdims=True)
    normed = (values * lax.rsqrt(mean_sq + norm_eps) * gain).astype(jnp.bfloat16)
    coef_in = sigma_scale / math.sqrt(block.shape[-1])
    coef_hidden = sigma_scale / math.sqrt(w_gate.shape[-1] * lax.axis_size("tp"))
    gate_wide = gate_right.astype(jnp.float32)[None]
    up_wide = up_right.astype(jnp.float32)[None]
    down_wide = down_right.astype(jnp.float32)[None]
    piece = lax.all_gather(normed, "tp", axis=0, tiled=True)
    gate = jnp.einsum("rkd,df->rkf", piece, w_gate, preferred_element_type=jnp.float32)
    gate_side = jnp.einsum("rkd,kd->rk", piece, gate_left, preferred_element_type=jnp.float32)
    gate = gate + coef_in * gate_side[:, :, None] * gate_wide
    upper = jnp.einsum("rkd,df->rkf", piece, w_up, preferred_element_type=jnp.float32)
    up_side = jnp.einsum("rkd,kd->rk", piece, up_left, preferred_element_type=jnp.float32)
    upper = upper + coef_in * up_side[:, :, None] * up_wide
    inner = (jax.nn.silu(gate) * upper).astype(jnp.bfloat16)
    term = jnp.einsum("rkf,fd->rkd", inner, w_down, preferred_element_type=jnp.float32)
    down_side = jnp.einsum("rkf,kf->rk", inner, down_left, preferred_element_type=jnp.float32)
    summed = lax.psum_scatter(
        (term + coef_hidden * down_side[:, :, None] * down_wide).astype(jnp.bfloat16),
        "tp",
        scatter_dimension=0,
        tiled=True,
    ).astype(jnp.float32)
    return (values + summed).astype(jnp.bfloat16)


def grouped_outer(fitness, left, right, groups):
    weighted = (fitness[:, None] * left.astype(jnp.float32)).reshape(groups, -1, left.shape[1])
    other = right.astype(jnp.float32).reshape(groups, -1, right.shape[1])
    parts = jnp.einsum("gmi,gmj->gij", weighted, other)
    rounded = lax.optimization_barrier(parts.astype(jnp.bfloat16)).astype(jnp.float32)
    return jnp.sum(rounded, axis=0)


def per_device(
    hidden_in,
    norm_gain,
    w_gate,
    w_up,
    w_down,
    gate_left,
    gate_right,
    up_left,
    up_right,
    down_left,
    down_right,
    ranks,
):
    seq_rows, members, width = hidden_in.shape
    sections = lax.axis_size("pp")
    section_index = lax.axis_index("pp")
    gain = norm_gain[0]
    gate_weight = w_gate[0]
    up_weight = w_up[0]
    down_weight = w_down[0]
    vectors = [gate_left[0], gate_right[0], up_left[0], up_right[0], down_left[0], down_right[0]]
    block_list = [(0, 0)]
    block_count = len(block_list)
    ticks = block_count + sections - 1
    output = jnp.zeros_like(hidden_in)
    arrived = jnp.zeros((seq_rows, members, width), jnp.bfloat16)
    for tick in range(ticks):
        if tick < block_count:
            own = hidden_in
        else:
            own = jnp.zeros_like(arrived)
        current = jnp.where(section_index == 0, own, arrived)
        position = tick - section_index
        picked = [vector for vector in vectors]
        result = feed_forward(
            current,
            gain,
            gate_weight,
            up_weight,
            down_weight,
            picked[0],
            picked[1],
            picked[2],
            picked[3],
            picked[4],
            picked[5],
        )
        valid = (position >= 0) & (position < block_count)
        before = output
        output = jnp.where(valid, result, before)
        if tick + 1 < ticks:
            arrived = from_behind(result, "pp", 1)
    pop_size = lax.axis_size("pop")
    population = members * pop_size
    all_ranks, all_gl, all_gr, all_ul, all_ur, all_dl, all_dr = (
        lax.all_gather(ranks, "pop", axis=0, tiled=True),
        *sent_together(
            (vectors[0], vectors[1], vectors[2], vectors[3], vectors[4], vectors[5]), "pop", 0, 1
        ),
    )
    fitness = (2.0 * all_ranks.astype(jnp.float32) / (population - 1) - 1.0) / math.sqrt(population)
    row_share = width // pop_size
    row_start = lax.axis_index("pop") * row_share
    own_gl = lax.dynamic_slice_in_dim(all_gl, row_start, row_share, 1)
    own_ul = lax.dynamic_slice_in_dim(all_ul, row_start, row_share, 1)
    own_dr = lax.dynamic_slice_in_dim(all_dr, row_start, row_share, 1)
    sum_gate = grouped_outer(fitness, own_gl, all_gr, pop_size)
    sum_up = grouped_outer(fitness, own_ul, all_ur, pop_size)
    sum_down = grouped_outer(fitness, all_dl, own_dr, pop_size)
    update_gate = sum_gate.astype(jnp.bfloat16)[None]
    update_up = sum_up.astype(jnp.bfloat16)[None]
    update_down = sum_down.astype(jnp.bfloat16)[None]
    return (output[None], update_gate, update_up, update_down)


def solution(mesh):
    placed = (
        P("tp", "pop", None),
        P("pp", None),
        P("pp", None, "tp"),
        P("pp", None, "tp"),
        P("pp", "tp", None),
        P("pp", "pop", None),
        P("pp", "pop", "tp"),
        P("pp", "pop", None),
        P("pp", "pop", "tp"),
        P("pp", "pop", "tp"),
        P("pp", "pop", None),
        P("pop"),
    )
    return jax.shard_map(
        per_device,
        mesh=mesh,
        in_specs=placed,
        out_specs=(
            P("pp", "tp", "pop", None),
            P("pp", "pop", "tp"),
            P("pp", "pop", "tp"),
            P("pp", "tp", "pop"),
        ),
        check_vma=False,
    )
```

profile of v0, /device:TPU:0, one launch (start us, length us, event | category | flops | bytes accessed | tf_op | source)
XLA Modules:
  0.0 329.0 jit_solution(4825222965416994438)
XLA Ops:
  7.2 1.3 fusion.20
  8.6 1.9 fusion.22
  10.5 0.7 bitcast_convert_fusion.1
  11.2 0.7 bitcast_convert_fusion
  12.0 53.0 %all-gather.4.cloned.1.call-done = bf16[256,2,4096]{2,0,1:T(8,128)(2,1)} async-done(((bf16[16,2,4096]{2,0,1:T(8,128)(2,1)}), bf16[256,2,4096]{2,0,1:T(8,128)(2,1)}) %all-gather.4.cloned.1.call-update) | async-done | bytes 4194320 | tf_op jit(solution)/shard_map/all_gather | solution.py:47
  64.9 3.5 %fusion.32 = f32[2,1,256]{2,1,0:T(1,128)S(1)} fusion(bf16[256,2,4096]{2,0,1:T(8,128)(2,1)} %all-gather.4.cloned.1.call-done, bf16[2,4096,1]{1,0,2:T(2,128)(2,1)} %bitcast.111), kind=kOutput, calls=%fused_computation.41 | convolution fusion | flops 4194304 | bytes 4212736 | tf_op jit(solution)/shard_map/rkd,kd->rk/dot_general | solution.py:52
  68.5 1.2 fusion.36
  69.7 5.6 %fusion.6 = f32[256,2,768]{2,0,1:T(8,128)S(1)} fusion(bf16[256,2,4096]{2,0,1:T(8,128)(2,1)S(1)} %copy-done, bf16[1,4096,768]{2,1,0:T(8,128)(2,1)} %param.15), kind=kOutput, calls=%fused_computation.8 | convolution fusion | flops 3221225472 | bytes 12058624 | tf_op jit(solution)/shard_map/rkd,df->rkf/dot_general | solution.py:51
  75.4 3.6 %multiply_convert_fusion.1 = bf16[256,2,768]{2,0,1:T(8,128)(2,1)S(1)} fusion(f32[256,2,768]{2,0,1:T(8,128)S(1)} %fusion.6, bf16[256,2,4096]{2,0,1:T(8,128)(2,1)S(1)} %copy-done, bf16[1,4096,768]{2,1,0:T(8,128)(2,1)S(1)} %bitcast.119, f32[2,768]{1,0:T(2,128)S(1)} %get-tuple-element.20, f32[256,2]{0,1:T(2,128)S(1)} %get-tuple-element.22, ...), kind=kOutput, calls=%fused_computation.18 | convolution fusion | flops 3225157632 | bytes 12861440 | tf_op jit(solution)/shard_map/rkd,df->rkf/dot_general | solution.py:48
  79.4 5.0 %add_convert_fusion.1 = bf16[256,2,4096]{2,0,1:T(8,128)(2,1)} fusion(bf16[256,2,768]{2,0,1:T(8,128)(2,1)S(1)} %multiply_convert_fusion.1, bf16[1,768,4096]{2,1,0:T(8,128)(2,1)S(1)} %bitcast.123, f32[2,4096]{1,0:T(2,128)S(1)} %bitcast_convert_fusion, f32[256,2]{0,1:T(2,128)S(1)} %fusion.45), kind=kOutput, calls=%fused_computation.1 | convolution fusion | flops 3227516928 | bytes 11307008 | tf_op jit(solution)/shard_map/rkf,fd->rkd/dot_general | solution.py:55
  84.5 77.5 %reduce-scatter.3.cloned.1.call-done = bf16[16,2,4096]{2,0,1:T(8,128)(2,1)} async-done(((bf16[256,2,4096]{2,0,1:T(8,128)(2,1)}), bf16[16,2,4096]{2,0,1:T(8,128)(2,1)}) %reduce-scatter.3.cloned.1.call-update) | async-done | bytes 262160 | tf_op jit(solution)/shard_map/reduce_scatter | solution.py:57
  162.0 1.1 fusion.23
  163.2 3.4 %collective-permute-start = (bf16[16,2,4096]{2,0,1:T(8,128)(2,1)S(1)}, bf16[16,2,4096]{2,0,1:T(8,128)(2,1)S(1)}, u32[]{:S(2)}, u32[]{:S(2)}) collective-permute-start(bf16[16,2,4096]{2,0,1:T(8,128)(2,1)S(1)} %fusion.23), channel_id=1, source_target_pairs={{0,1},{2,3},{4,5},{6,7},{8,9},{10,11},{12,13},{14,15},{16,17},{18,... | collective-permute-start | bytes 786440 | tf_op jit(solution)/shard_map/ppermute | solution.py:14
  166.5 3.9 %collective-permute-done = bf16[16,2,4096]{2,0,1:T(8,128)(2,1)S(1)} collective-permute-done((bf16[16,2,4096]{2,0,1:T(8,128)(2,1)S(1)}, bf16[16,2,4096]{2,0,1:T(8,128)(2,1)S(1)}, u32[]{:S(2)}, u32[]{:S(2)}) %collective-permute-start) | collective-permute-done | bytes 262176 | tf_op jit(solution)/shard_map/ppermute | solution.py:14
  170.6 0.8 fusion.26
  171.7 51.6 %all-gather.6.cloned.1.call-done = bf16[256,2,4096]{2,0,1:T(8,128)(2,1)} async-done(((bf16[16,2,4096]{2,0,1:T(8,128)(2,1)}), bf16[256,2,4096]{2,0,1:T(8,128)(2,1)}) %all-gather.6.cloned.1.call-update) | async-done | bytes 4194320 | tf_op jit(solution)/shard_map/all_gather | solution.py:47
  223.4 3.5 %fusion.30 = f32[2,1,256]{2,1,0:T(1,128)S(1)} fusion(bf16[256,2,4096]{2,0,1:T(8,128)(2,1)} %all-gather.6.cloned.1.call-done, bf16[2,4096,1]{1,0,2:T(2,128)(2,1)S(1)} %bitcast.112), kind=kOutput, calls=%fused_computation.39 | convolution fusion | flops 4194304 | bytes 4212736 | tf_op jit(solution)/shard_map/rkd,kd->rk/dot_general | solution.py:52
  226.9 1.2 fusion.34
  228.1 5.6 %fusion.4 = f32[256,2,768]{2,0,1:T(8,128)S(1)} fusion(bf16[256,2,4096]{2,0,1:T(8,128)(2,1)S(1)} %copy-done.1, bf16[1,4096,768]{2,1,0:T(8,128)(2,1)} %param.15), kind=kOutput, calls=%fused_computation.6 | convolution fusion | flops 3221225472 | bytes 12058624 | tf_op jit(solution)/shard_map/rkd,df->rkf/dot_general | solution.py:51
  233.8 3.6 %multiply_convert_fusion = bf16[256,2,768]{2,0,1:T(8,128)(2,1)S(1)} fusion(f32[256,2,768]{2,0,1:T(8,128)S(1)} %fusion.4, bf16[256,2,4096]{2,0,1:T(8,128)(2,1)S(1)} %copy-done.1, bf16[1,4096,768]{2,1,0:T(8,128)(2,1)S(1)} %bitcast.121, f32[256,2]{0,1:T(2,128)S(1)} %fusion.43, f32[256,2]{0,1:T(2,128)S(1)} %fusion.44, f32[2,768]{1,0:T(2,128)S(1)} %get-tuple-element.20, ...), kind=kOutput, calls=%fused_computation.17 | convolution fusion | flops 3225157632 | bytes 12861440 | tf_op jit(solution)/shard_map/rkd,df->rkf/dot_general | solution.py:48
  237.8 5.0 %add_convert_fusion = bf16[256,2,4096]{2,0,1:T(8,128)(2,1)} fusion(bf16[256,2,768]{2,0,1:T(8,128)(2,1)S(1)} %multiply_convert_fusion, bf16[1,768,4096]{2,1,0:T(8,128)(2,1)S(1)} %bitcast.125, f32[256,2]{0,1:T(2,128)S(1)} %fusion.42, f32[2,4096]{1,0:T(2,128)S(1)} %bitcast_convert_fusion), kind=kOutput, calls=%fused_computation | convolution fusion | flops 3227516928 | bytes 11307008 | tf_op jit(solution)/shard_map/rkf,fd->rkd/dot_general | solution.py:55
  245.0 6.4 %all-reduce = s32[8]{0:T(128)S(1)} all-reduce(s32[8]{0:T(128)S(1)} %dynamic-update-slice), channel_id=1, replica_groups=mesh['pop'=4,'tp'=16,'pp'=2] {'pop'}, use_global_device_ids=true, to_apply=%add | all-reduce | flops 8 | bytes 64
  251.5 7.4 %all-gather = bf16[4,2,14592]{2,1,0:T(2,128)(2,1)S(1)} all-gather(bf16[1,2,14592]{2,1,0:T(2,128)(2,1)S(1)} %bitcast.113), channel_id=1, replica_groups=mesh['pop'=4,'tp'=16,'pp'=2] {'pop'}, dimensions={0}, use_global_device_ids=true | all-gather | bytes 291840 | tf_op jit(solution)/shard_map/all_gather | solution.py:19
  259.4 4.5 %fusion.49 = bf16[4,768,1024]{2,1,0:T(8,128)(2,1)} fusion(bf16[4,2,768]{2,1,0:T(2,128)(2,1)S(1)} %reshape.60, bf16[4,2,1024]{2,1,0:T(2,128)(2,1)S(1)} %reshape.61), kind=kOutput, calls=%fused_computation.78 | convolution fusion | flops 12582912 | bytes 6320128 | tf_op jit(solution)/shard_map/gmi,gmj->gij/dot_general | solution.py:69
  263.8 4.5 %fusion.51 = bf16[4,1024,768]{2,1,0:T(8,128)(2,1)} fusion(bf16[4,2,1024]{2,1,0:T(2,128)(2,1)S(1)} %reshape.56, bf16[4,2,768]{2,1,0:T(2,128)(2,1)S(1)} %reshape.57), kind=kOutput, calls=%fused_computation.80 | convolution fusion | flops 12582912 | bytes 6320128 | tf_op jit(solution)/shard_map/gmi,gmj->gij/dot_general | solution.py:69
  268.3 6.0 %reduce_sum.58 = bf16[768,1024]{1,0:T(8,128)(2,1)} reduce(bf16[4,768,1024]{2,1,0:T(8,128)(2,1)} %fusion.49, bf16[]{:T(256)} %constant.15.clone.1), dimensions={0}, to_apply=%region_6.7 | reduce | flops 2359296 | bytes 7864322 | tf_op jit(solution)/shard_map/reduce_sum | solution.py:71
  274.3 5.4 %reduce_sum.56 = bf16[1024,768]{1,0:T(8,128)(2,1)} reduce(bf16[4,1024,768]{2,1,0:T(8,128)(2,1)} %fusion.51, bf16[]{:T(256)} %constant.15.clone.1), dimensions={0}, to_apply=%region_4.5 | reduce | flops 2359296 | bytes 7864322 | tf_op jit(solution)/shard_map/reduce_sum | solution.py:71
  279.7 4.5 %fusion.50 = bf16[4,1024,768]{2,1,0:T(8,128)(2,1)} fusion(bf16[4,2,1024]{2,1,0:T(2,128)(2,1)S(1)} %reshape.58, bf16[4,2,768]{2,1,0:T(2,128)(2,1)S(1)} %reshape.59), kind=kOutput, calls=%fused_computation.79 | convolution fusion | flops 12582912 | bytes 6320128 | tf_op jit(solution)/shard_map/gmi,gmj->gij/dot_general | solution.py:69
  284.2 5.3 %reduce_sum.57 = bf16[1024,768]{1,0:T(8,128)(2,1)} reduce(bf16[4,1024,768]{2,1,0:T(8,128)(2,1)} %fusion.50, bf16[]{:T(256)} %constant.15.clone.1), dimensions={0}, to_apply=%region_5.6 | reduce | flops 2359296 | bytes 7864322 | tf_op jit(solution)/shard_map/reduce_sum | solution.py:71
  289.5 30.8 %reduce-scatter.5.cloned.1.call-done = bf16[16,2,4096]{2,0,1:T(8,128)(2,1)} async-done(((bf16[256,2,4096]{2,0,1:T(8,128)(2,1)}), bf16[16,2,4096]{2,0,1:T(8,128)(2,1)}) %reduce-scatter.5.cloned.1.call-update) | async-done | bytes 262160 | tf_op jit(solution)/shard_map/reduce_scatter | solution.py:57
  320.4 1.1 fusion.29
  321.5 1.0 copy.19
  (82 shorter events, 3.2 us)
Async XLA Ops:
  7.2 61.3 %copy-start.3 = (bf16[1,2,4096]{2,1,0:T(2,128)(2,1)S(1)}, bf16[1,2,4096]{2,1,0:T(2,128)(2,1)}, u32[]{:S(2)}) copy-start(bf16[1,2,4096]{2,1,0:T(2,128)(2,1)} %param.17) | copy-start | bytes 49156
  7.2 57.8 %all-gather.4.cloned.1.call-start = ((), (), s32[]{:S(2)}) async-start(), calls=%async_computation.2 | async-start | bytes 4456448 | tf_op jit(solution)/shard_map/all_gather | solution.py:47
  10.5 151.6 %reduce-scatter.3.cloned.1.call-start = ((), (), s32[]{:S(2)}) async-start(), calls=%async_computation.3 | async-start | bytes 4456448 | tf_op jit(solution)/shard_map/reduce_scatter | solution.py:57
  64.9 3.5 %copy-start = (bf16[256,2,4096]{2,0,1:T(8,128)(2,1)S(1)}, bf16[256,2,4096]{2,0,1:T(8,128)(2,1)}, u32[]{:S(2)}) copy-start(bf16[256,2,4096]{2,0,1:T(8,128)(2,1)} %all-gather.4.cloned.1.call-done) | copy-start | bytes 12582916
  68.5 6.9 %slice-start = ((s8[6291456]{0:T(1024)(128)(4,1)}), s8[4194304]{0:T(1024)(128)(4,1)S(1)}, s32[]{:S(2)}) async-start(s8[6291456]{0:T(1024)(128)(4,1)} %bitcast.118), calls=%async_computation.6 | async-start | bytes 8388608
  69.7 5.7 %slice-start.1 = ((s8[6291456]{0:T(1024)(128)(4,1)}), s8[2097152]{0:T(1024)(128)(4,1)S(1)}, s32[]{:S(2)}) async-start(s8[6291456]{0:T(1024)(128)(4,1)} %bitcast.118), calls=%async_computation.7 | async-start | bytes 4194304
  69.7 9.7 %slice-start.4 = ((s8[6291456]{0:T(1024)(128)(4,1)}), s8[4194304]{0:T(1024)(128)(4,1)S(1)}, s32[]{:S(2)}) async-start(s8[6291456]{0:T(1024)(128)(4,1)} %bitcast.122), calls=%async_computation.10 | async-start | bytes 8388608
  75.4 3.7 %copy-start.5 = (bf16[1,2,768]{2,1,0:T(2,128)(2,1)S(1)}, bf16[1,2,768]{2,1,0:T(2,128)(2,1)}, u32[]{:S(2)}) copy-start(bf16[1,2,768]{2,1,0:T(2,128)(2,1)} %param.21) | copy-start | bytes 9220
  75.4 4.0 %slice-start.5 = ((s8[6291456]{0:T(1024)(128)(4,1)}), s8[2097152]{0:T(1024)(128)(4,1)S(1)}, s32[]{:S(2)}) async-start(s8[6291456]{0:T(1024)(128)(4,1)} %bitcast.122), calls=%async_computation.11 | async-start | bytes 4194304
  84.4 77.6 %copy-start.2 = (bf16[16,2,4096]{2,1,0:T(2,128)(2,1)S(1)}, bf16[16,2,4096]{2,1,0:T(2,128)(2,1)}, u32[]{:S(2)}) copy-start(bf16[16,2,4096]{2,1,0:T(2,128)(2,1)} %param.12) | copy-start | bytes 786436
  84.4 86.2 %copy-start.6 = (f32[1,4096]{1,0:T(1,128)S(1)}, f32[1,4096]{1,0:T(1,128)}, u32[]{:S(2)}) copy-start(f32[1,4096]{1,0:T(1,128)} %param.13) | copy-start | bytes 49156
  84.4 138.9 %copy-start.4 = (bf16[1,2,4096]{2,1,0:T(2,128)(2,1)S(1)}, bf16[1,2,4096]{2,1,0:T(2,128)(2,1)}, u32[]{:S(2)}) copy-start(bf16[1,2,4096]{2,1,0:T(2,128)(2,1)} %param.19) | copy-start | bytes 49156
  84.5 138.9 %all-gather.6.cloned.1.call-start = ((), (), s32[]{:S(2)}) async-start(), calls=%async_computation.4 | async-start | bytes 4456448 | tf_op jit(solution)/shard_map/all_gather | solution.py:47
  163.2 7.3 %collective-permute-start = (bf16[16,2,4096]{2,0,1:T(8,128)(2,1)S(1)}, bf16[16,2,4096]{2,0,1:T(8,128)(2,1)S(1)}, u32[]{:S(2)}, u32[]{:S(2)}) collective-permute-start(bf16[16,2,4096]{2,0,1:T(8,128)(2,1)S(1)} %fusion.23), channel_id=1, source_target_pairs={{0,1},{2,3},{4,5},{6,7},{8,9},{10,11},{12,13},{14,15},{16,17},{18,... | collective-permute-start | bytes 786440 | tf_op jit(solution)/shard_map/ppermute | solution.py:14
  171.5 148.9 %reduce-scatter.5.cloned.1.call-start = ((), (), s32[]{:S(2)}) async-start(), calls=%async_computation.5 | async-start | bytes 4456448 | tf_op jit(solution)/shard_map/reduce_scatter | solution.py:57
  223.4 3.5 %copy-start.1 = (bf16[256,2,4096]{2,0,1:T(8,128)(2,1)S(1)}, bf16[256,2,4096]{2,0,1:T(8,128)(2,1)}, u32[]{:S(2)}) copy-start(bf16[256,2,4096]{2,0,1:T(8,128)(2,1)} %all-gather.6.cloned.1.call-done) | copy-start | bytes 12582916
  226.9 6.9 %slice-start.2 = ((s8[6291456]{0:T(1024)(128)(4,1)}), s8[4194304]{0:T(1024)(128)(4,1)S(1)}, s32[]{:S(2)}) async-start(s8[6291456]{0:T(1024)(128)(4,1)} %bitcast.120), calls=%async_computation.8 | async-start | bytes 8388608
  228.1 5.7 %slice-start.3 = ((s8[6291456]{0:T(1024)(128)(4,1)}), s8[2097152]{0:T(1024)(128)(4,1)S(1)}, s32[]{:S(2)}) async-start(s8[6291456]{0:T(1024)(128)(4,1)} %bitcast.120), calls=%async_computation.9 | async-start | bytes 4194304
  228.1 9.7 %slice-start.6 = ((s8[6291456]{0:T(1024)(128)(4,1)}), s8[4194304]{0:T(1024)(128)(4,1)S(1)}, s32[]{:S(2)}) async-start(s8[6291456]{0:T(1024)(128)(4,1)} %bitcast.124), calls=%async_computation.12 | async-start | bytes 8388608
  233.8 4.0 %slice-start.7 = ((s8[6291456]{0:T(1024)(128)(4,1)}), s8[2097152]{0:T(1024)(128)(4,1)S(1)}, s32[]{:S(2)}) async-start(s8[6291456]{0:T(1024)(128)(4,1)} %bitcast.124), calls=%async_computation.13 | async-start | bytes 4194304
  242.8 0.7 copy-start.11
  242.8 1.9 copy-start.10
  242.8 8.6 %copy-start.8 = (bf16[1,2,768]{2,1,0:T(2,128)(2,1)S(1)}, bf16[1,2,768]{2,1,0:T(2,128)(2,1)}, u32[]{:S(2)}) copy-start(bf16[1,2,768]{2,1,0:T(2,128)(2,1)} %param.18) | copy-start | bytes 9220
  242.8 8.6 %copy-start.9 = (bf16[1,2,768]{2,1,0:T(2,128)(2,1)S(1)}, bf16[1,2,768]{2,1,0:T(2,128)(2,1)}, u32[]{:S(2)}) copy-start(bf16[1,2,768]{2,1,0:T(2,128)(2,1)} %param.20) | copy-start | bytes 9220
  242.8 8.7 %copy-start.7 = (bf16[1,2,4096]{2,1,0:T(2,128)(2,1)S(1)}, bf16[1,2,4096]{2,1,0:T(2,128)(2,1)}, u32[]{:S(2)}) copy-start(bf16[1,2,4096]{2,1,0:T(2,128)(2,1)} %param.22) | copy-start | bytes 49156
Sparse Core Ops, SparseCore 0:
  10.7 54.1 all-gather.3
  84.6 77.3 reduce-scatter.2
  171.6 51.7 all-gather.5
  243.0 77.3 reduce-scatter.4
where the time goes:
time: 329 us
  waiting for transfers between devices  217 us (66%)
  matrix products  52.1 us (16%)
  other arithmetic  24.7 us (8%)
  between operations  14.8 us (4%)
  blocking collectives  13.9 us (4%)
  starting transfers between devices  3.72 us (1%)
    reduce_scatter x2, waiting for transfers between devices, feed_forward(): lax.psum_scatter((term + coef_hidden * down_side[:, :, None] * down_wide)...  108 us
    all_gather x2, waiting for transfers between devices, feed_forward(): piece = lax.all_gather(normed, 'tp', axis=0, tiled=True)  105 us
    reduce_sum x3, other arithmetic, grouped_outer(): return jnp.sum(rounded, axis=0)  16.7 us
    dot_general x3, matrix products, grouped_outer(): parts = jnp.einsum('gmi,gmj->gij', weighted, other)  13.4 us
    dot_general x2, matrix products, feed_forward(): jnp.einsum('rkd,df->rkf', piece, w_up, preferred_element_type=jnp.float32)  11.3 us
    dot_general x2, matrix products, feed_forward(): jnp.einsum('rkf,fd->rkd', inner, w_down, preferred_element_type=jnp.float32)  10.1 us
    all_gather x1, blocking collectives, sent_together(): out, at, done = (lax.all_gather(both, axis, axis=dim, tiled=True), 0, [])  7.43 us
    dot_general x2, matrix products, feed_forward(): jnp.einsum('rkd,df->rkf', piece, w_gate, preferred_element_type=jnp.float32)  7.28 us
  transfers between devices with their start and end apart: 5, of which 5 were waited for; matrix products, arithmetic and copies ran while one was open for 10% of the time, Pallas kernels for 0%

commit v1 on v0

--- a/solution.py
+++ b/solution.py
@@ -6,6 +6,27 @@
 
 sigma_scale = 0.3
 norm_eps = 1e-05
+
+
+def ring_gather(value, axis, dim):
+    length, index, rows = (lax.axis_size(axis), lax.axis_index(axis), value.shape[dim])
+    right = [(i, (i + 1) % length) for i in range(length)]
+    downward = [(i, (i - 1) % length) for i in range(length)]
+    out = jnp.zeros((*value.shape[:dim], length * rows, *value.shape[dim + 1 :]), value.dtype)
+    out = lax.dynamic_update_slice_in_dim(out, value, index * rows, axis=dim)
+    from_left = from_right = value
+    halfway = length // 2
+    for step in range(1, halfway + 1):
+        from_left = lax.ppermute(from_left, axis, right)
+        out = lax.dynamic_update_slice_in_dim(
+            out, from_left, (index - step) % length * rows, axis=dim
+        )
+        if step < length - halfway:
+            from_right = lax.ppermute(from_right, axis, downward)
+            out = lax.dynamic_update_slice_in_dim(
+                out, from_right, (index + step) % length * rows, axis=dim
+            )
+    return out
 
 
 def from_behind(block, axis, distance):
@@ -44,7 +65,7 @@
     gate_wide = gate_right.astype(jnp.float32)[None]
     up_wide = up_right.astype(jnp.float32)[None]
     down_wide = down_right.astype(jnp.float32)[None]
-    piece = lax.all_gather(normed, "tp", axis=0, tiled=True)
+    piece = ring_gather(normed, "tp", 0)
     gate = jnp.einsum("rkd,df->rkf", piece, w_gate, preferred_element_type=jnp.float32)
     gate_side = jnp.einsum("rkd,kd->rk", piece, gate_left, preferred_element_type=jnp.float32)
     gate = gate + coef_in * gate_side[:, :, None] * gate_wide

time: 329 us -> 394 us (1.20); the launches traced: 329 us -> 388 us
  starting transfers between devices: 3.72 us -> 82.1 us
  waiting for transfers between devices: 217 us -> 185 us
  local copies, waits for them, and re-layouts: 2.85 us -> 17.1 us
    all_gather x2 -> x0, waiting for transfers between devices: 105 us -> none  [feed_forward(): piece = lax.all_gather(normed, 'tp', axis=0, tiled=True)]
    ppermute x0 -> x30, starting transfers between devices: none -> 78.6 us  [the longest x14 75.1 us: ring_gather(): from_right = lax.ppermute(from_right, axis, downward)]
    ppermute x0 -> x30, waiting for transfers between devices: none -> 78 us  [the longest x16 76.9 us: ring_gather(): from_left = lax.ppermute(from_left, axis, right)]
    dynamic_update_slice x0 -> x30, local copies, waits for them, and re-layouts: none -> 11.2 us  [the longest x16 6 us: ring_gather(): lax.dynamic_update_slice_in_dim(out, from_left, (index - step) % length *...]
    reduce_scatter x2, waiting for transfers between devices: 108 us -> 103 us  [feed_forward(): lax.psum_scatter((term + coef_hidden * down_side[:, :, None] * down_wide)...]
  transfers between devices with their start and end apart: 5 -> 33, of which waited for: 5 -> 22; matrix products, arithmetic and copies ran while one was open for 10% -> 11% of each run, Pallas kernels for 0% -> 0%
where the time goes in v1:
time: 394 us; the launch traced here: 388 us
  waiting for transfers between devices  185 us (47%)
  starting transfers between devices  82.1 us (21%)
  matrix products  52 us (13%)
  other arithmetic  21.9 us (6%)
  local copies, waits for them, and re-layouts  17.1 us (4%)
  between operations  15.7 us (4%)
  blocking collectives  13.5 us (3%)
    reduce_scatter x2, waiting for transfers between devices, feed_forward(): lax.psum_scatter((term + coef_hidden * down_side[:, :, None] * down_wide)...  103 us
    ppermute x16, waiting for transfers between devices, ring_gather(): from_left = lax.ppermute(from_left, axis, right)  76.9 us
    ppermute x14, starting transfers between devices, ring_gather(): from_right = lax.ppermute(from_right, axis, downward)  75.1 us
    reduce_sum x3, other arithmetic, grouped_outer(): return jnp.sum(rounded, axis=0)  16.9 us
    dot_general x3, matrix products, grouped_outer(): parts = jnp.einsum('gmi,gmj->gij', weighted, other)  13.5 us
    dot_general x2, matrix products, feed_forward(): jnp.einsum('rkf,fd->rkd', inner, w_down, preferred_element_type=jnp.float32)  10.2 us
    dot_general x2, matrix products, feed_forward(): jnp.einsum('rkd,df->rkf', piece, w_up, preferred_element_type=jnp.float32)  9.53 us
    dot_general x2, matrix products, feed_forward(): jnp.einsum('rkd,df->rkf', piece, w_gate, preferred_element_type=jnp.float32)  8.77 us
  transfers between devices with their start and end apart: 33, of which 22 were waited for; matrix products, arithmetic and copies ran while one was open for 11% of the time, Pallas kernels for 0%

profile of v1, /device:TPU:0, one launch (start us, length us, event | category | flops | bytes accessed | tf_op | source)
XLA Modules:
  0.0 387.7 jit_solution(1927474539770059098)
XLA Ops:
  13.7 4.7 %collective-permute-start.1 = (bf16[16,2,4096]{2,0,1:T(8,128)(2,1)S(1)}, bf16[16,2,4096]{2,0,1:T(8,128)(2,1)S(1)}, u32[]{:S(2)}, u32[]{:S(2)}) collective-permute-start(bf16[16,2,4096]{2,0,1:T(8,128)(2,1)S(1)} %get-tuple-element.15), channel_id=1, source_target_pairs={{0,30},{2,0},{4,2},{6,4},{8,6},{10,8},{12,10},{14,12},{16,14},{18,... | collective-permute-start | bytes 786440 | tf_op jit(solution)/shard_map/ppermute | solution.py:25
  18.7 6.0 %collective-permute-done = bf16[16,2,4096]{2,0,1:T(8,128)(2,1)S(1)} collective-permute-done((bf16[16,2,4096]{2,0,1:T(8,128)(2,1)S(1)}, bf16[16,2,4096]{2,0,1:T(8,128)(2,1)S(1)}, u32[]{:S(2)}, u32[]{:S(2)}) %collective-permute-start) | collective-permute-done | bytes 262176 | tf_op jit(solution)/shard_map/ppermute | solution.py:20
  24.7 5.3 %collective-permute-start.3 = (bf16[16,2,4096]{2,0,1:T(8,128)(2,1)S(1)}, bf16[16,2,4096]{2,0,1:T(8,128)(2,1)S(1)}, u32[]{:S(2)}, u32[]{:S(2)}) collective-permute-start(bf16[16,2,4096]{2,0,1:T(8,128)(2,1)S(1)} %collective-permute-done.1), channel_id=1, source_target_pairs={{0,30},{2,0},{4,2},{6,4},{8,6},{10,8},{12,10},{14,12},{16,14},{18,... | collective-permute-start | bytes 786440 | tf_op jit(solution)/shard_map/ppermute | solution.py:25
  35.5 5.3 %collective-permute-start.5 = (bf16[16,2,4096]{2,0,1:T(8,128)(2,1)S(1)}, bf16[16,2,4096]{2,0,1:T(8,128)(2,1)S(1)}, u32[]{:S(2)}, u32[]{:S(2)}) collective-permute-start(bf16[16,2,4096]{2,0,1:T(8,128)(2,1)S(1)} %collective-permute-done.3), channel_id=1, source_target_pairs={{0,30},{2,0},{4,2},{6,4},{8,6},{10,8},{12,10},{14,12},{16,14},{18,... | collective-permute-start | bytes 786440 | tf_op jit(solution)/shard_map/ppermute | solution.py:25
  45.4 5.3 %collective-permute-start.7 = (bf16[16,2,4096]{2,0,1:T(8,128)(2,1)S(1)}, bf16[16,2,4096]{2,0,1:T(8,128)(2,1)S(1)}, u32[]{:S(2)}, u32[]{:S(2)}) collective-permute-start(bf16[16,2,4096]{2,0,1:T(8,128)(2,1)S(1)} %collective-permute-done.5), channel_id=1, source_target_pairs={{0,30},{2,0},{4,2},{6,4},{8,6},{10,8},{12,10},{14,12},{16,14},{18,... | collective-permute-start | bytes 786440 | tf_op jit(solution)/shard_map/ppermute | solution.py:25
  55.1 5.3 %collective-permute-start.9 = (bf16[16,2,4096]{2,0,1:T(8,128)(2,1)S(1)}, bf16[16,2,4096]{2,0,1:T(8,128)(2,1)S(1)}, u32[]{:S(2)}, u32[]{:S(2)}) collective-permute-start(bf16[16,2,4096]{2,0,1:T(8,128)(2,1)S(1)} %collective-permute-done.7), channel_id=1, source_target_pairs={{0,30},{2,0},{4,2},{6,4},{8,6},{10,8},{12,10},{14,12},{16,14},{18,... | collective-permute-start | bytes 786440 | tf_op jit(solution)/shard_map/ppermute | solution.py:25
  64.8 5.3 %collective-permute-start.11 = (bf16[16,2,4096]{2,0,1:T(8,128)(2,1)S(1)}, bf16[16,2,4096]{2,0,1:T(8,128)(2,1)S(1)}, u32[]{:S(2)}, u32[]{:S(2)}) collective-permute-start(bf16[16,2,4096]{2,0,1:T(8,128)(2,1)S(1)} %collective-permute-done.9), channel_id=1, source_target_pairs={{0,30},{2,0},{4,2},{6,4},{8,6},{10,8},{12,10},{14,12},{16,14},{18,... | collective-permute-start | bytes 786440 | tf_op jit(solution)/shard_map/ppermute | solution.py:25
  74.5 5.6 %collective-permute-start.13 = (bf16[16,2,4096]{2,0,1:T(8,128)(2,1)S(1)}, bf16[16,2,4096]{2,0,1:T(8,128)(2,1)S(1)}, u32[]{:S(2)}, u32[]{:S(2)}) collective-permute-start(bf16[16,2,4096]{2,0,1:T(8,128)(2,1)S(1)} %collective-permute-done.11), channel_id=1, source_target_pairs={{0,30},{2,0},{4,2},{6,4},{8,6},{10,8},{12,10},{14,12},{16,14},{18,... | collective-permute-start | bytes 786440 | tf_op jit(solution)/shard_map/ppermute | solution.py:25
  86.8 8.2 %collective-permute-done.14 = bf16[16,2,4096]{2,0,1:T(8,128)(2,1)S(1)} collective-permute-done((bf16[16,2,4096]{2,0,1:T(8,128)(2,1)S(1)}, bf16[16,2,4096]{2,0,1:T(8,128)(2,1)S(1)}, u32[]{:S(2)}, u32[]{:S(2)}) %collective-permute-start.14) | collective-permute-done | bytes 262176 | tf_op jit(solution)/shard_map/ppermute | solution.py:20
  102.9 5.4 %fusion.10 = f32[256,2,768]{2,0,1:T(8,128)S(1)} fusion(bf16[256,2,4096]{2,0,1:T(8,128)(2,1)} %constant_dynamic-update-slice_fusion.19, bf16[1,4096,768]{2,1,0:T(8,128)(2,1)S(1)} %bitcast.119), kind=kOutput, calls=%fused_computation.12 | convolution fusion | flops 3221225472 | bytes 12058624 | tf_op jit(solution)/shard_map/rkd,df->rkf/dot_general | solution.py:69
  108.3 5.9 %multiply_convert_fusion.1 = bf16[256,2,768]{2,0,1:T(8,128)(2,1)S(1)} fusion(f32[256,2,768]{2,0,1:T(8,128)S(1)} %fusion.10, bf16[256,2,4096]{2,0,1:T(8,128)(2,1)} %constant_dynamic-update-slice_fusion.19, bf16[1,4096,768]{2,1,0:T(8,128)(2,1)S(1)} %bitcast.123, f32[2,768]{1,0:T(2,128)S(1)} %get-tuple-element.24, f32[256,2]{0,1:T(2,128)S(1)} %get-tuple-element.26, ...), kind=kOutput, calls=%fused_computation.18 | convolution fusion | flops 3225157632 | bytes 12861440 | tf_op jit(solution)/shard_map/rkd,df->rkf/dot_general | solution.py:72
  114.6 5.1 %add_convert_fusion.1 = bf16[256,2,4096]{2,0,1:T(8,128)(2,1)} fusion(bf16[256,2,768]{2,0,1:T(8,128)(2,1)S(1)} %multiply_convert_fusion.1, bf16[1,768,4096]{2,1,0:T(8,128)(2,1)S(1)} %bitcast.127, f32[2,4096]{1,0:T(2,128)S(1)} %bitcast_convert_fusion, f32[256,2]{0,1:T(2,128)S(1)} %fusion.45), kind=kOutput, calls=%fused_computation.1 | convolution fusion | flops 3227516928 | bytes 11307008 | tf_op jit(solution)/shard_map/rkf,fd->rkd/dot_general | solution.py:76
  119.8 74.4 %reduce-scatter.3.cloned.1.call-done = bf16[16,2,4096]{2,0,1:T(8,128)(2,1)} async-done(((bf16[256,2,4096]{2,0,1:T(8,128)(2,1)}), bf16[16,2,4096]{2,0,1:T(8,128)(2,1)}) %reduce-scatter.3.cloned.1.call-update) | async-done | bytes 262160 | tf_op jit(solution)/shard_map/reduce_scatter | solution.py:78
  213.2 5.4 %collective-permute-start.19 = (bf16[16,2,4096]{2,0,1:T(8,128)(2,1)S(1)}, bf16[16,2,4096]{2,0,1:T(8,128)(2,1)S(1)}, u32[]{:S(2)}, u32[]{:S(2)}) collective-permute-start(bf16[16,2,4096]{2,0,1:T(8,128)(2,1)S(1)} %collective-permute-done.17), channel_id=1, source_target_pairs={{0,30},{2,0},{4,2},{6,4},{8,6},{10,8},{12,10},{14,12},{16,14},{18,... | collective-permute-start | bytes 786440 | tf_op jit(solution)/shard_map/ppermute | solution.py:25
  222.9 5.4 %collective-permute-start.21 = (bf16[16,2,4096]{2,0,1:T(8,128)(2,1)S(1)}, bf16[16,2,4096]{2,0,1:T(8,128)(2,1)S(1)}, u32[]{:S(2)}, u32[]{:S(2)}) collective-permute-start(bf16[16,2,4096]{2,0,1:T(8,128)(2,1)S(1)} %collective-permute-done.19), channel_id=1, source_target_pairs={{0,30},{2,0},{4,2},{6,4},{8,6},{10,8},{12,10},{14,12},{16,14},{18,... | collective-permute-start | bytes 786440 | tf_op jit(solution)/shard_map/ppermute | solution.py:25
  232.7 5.7 %collective-permute-start.23 = (bf16[16,2,4096]{2,0,1:T(8,128)(2,1)S(1)}, bf16[16,2,4096]{2,0,1:T(8,128)(2,1)S(1)}, u32[]{:S(2)}, u32[]{:S(2)}) collective-permute-start(bf16[16,2,4096]{2,0,1:T(8,128)(2,1)S(1)} %collective-permute-done.21), channel_id=1, source_target_pairs={{0,30},{2,0},{4,2},{6,4},{8,6},{10,8},{12,10},{14,12},{16,14},{18,... | collective-permute-start | bytes 786440 | tf_op jit(solution)/shard_map/ppermute | solution.py:25
  238.4 5.0 %collective-permute-done.22 = bf16[16,2,4096]{2,0,1:T(8,128)(2,1)S(1)} collective-permute-done((bf16[16,2,4096]{2,0,1:T(8,128)(2,1)S(1)}, bf16[16,2,4096]{2,0,1:T(8,128)(2,1)S(1)}, u32[]{:S(2)}, u32[]{:S(2)}) %collective-permute-start.22) | collective-permute-done | bytes 262176 | tf_op jit(solution)/shard_map/ppermute | solution.py:20
  243.9 5.8 %collective-permute-start.25 = (bf16[16,2,4096]{2,0,1:T(8,128)(2,1)S(1)}, bf16[16,2,4096]{2,0,1:T(8,128)(2,1)S(1)}, u32[]{:S(2)}, u32[]{:S(2)}) collective-permute-start(bf16[16,2,4096]{2,0,1:T(8,128)(2,1)S(1)} %collective-permute-done.23), channel_id=1, source_target_pairs={{0,30},{2,0},{4,2},{6,4},{8,6},{10,8},{12,10},{14,12},{16,14},{18,... | collective-permute-start | bytes 786440 | tf_op jit(solution)/shard_map/ppermute | solution.py:25
  249.7 6.1 %collective-permute-done.24 = bf16[16,2,4096]{2,0,1:T(8,128)(2,1)S(1)} collective-permute-done((bf16[16,2,4096]{2,0,1:T(8,128)(2,1)S(1)}, bf16[16,2,4096]{2,0,1:T(8,128)(2,1)S(1)}, u32[]{:S(2)}, u32[]{:S(2)}) %collective-permute-start.24) | collective-permute-done | bytes 262176 | tf_op jit(solution)/shard_map/ppermute | solution.py:20
  256.3 5.8 %collective-permute-start.27 = (bf16[16,2,4096]{2,0,1:T(8,128)(2,1)S(1)}, bf16[16,2,4096]{2,0,1:T(8,128)(2,1)S(1)}, u32[]{:S(2)}, u32[]{:S(2)}) collective-permute-start(bf16[16,2,4096]{2,0,1:T(8,128)(2,1)S(1)} %collective-permute-done.25), channel_id=1, source_target_pairs={{0,30},{2,0},{4,2},{6,4},{8,6},{10,8},{12,10},{14,12},{16,14},{18,... | collective-permute-start | bytes 786440 | tf_op jit(solution)/shard_map/ppermute | solution.py:25
  262.1 5.4 %collective-permute-done.26 = bf16[16,2,4096]{2,0,1:T(8,128)(2,1)S(1)} collective-permute-done((bf16[16,2,4096]{2,0,1:T(8,128)(2,1)S(1)}, bf16[16,2,4096]{2,0,1:T(8,128)(2,1)S(1)}, u32[]{:S(2)}, u32[]{:S(2)}) %collective-permute-start.26) | collective-permute-done | bytes 262176 | tf_op jit(solution)/shard_map/ppermute | solution.py:20
  267.9 5.8 %collective-permute-start.29 = (bf16[16,2,4096]{2,0,1:T(8,128)(2,1)S(1)}, bf16[16,2,4096]{2,0,1:T(8,128)(2,1)S(1)}, u32[]{:S(2)}, u32[]{:S(2)}) collective-permute-start(bf16[16,2,4096]{2,0,1:T(8,128)(2,1)S(1)} %collective-permute-done.27), channel_id=1, source_target_pairs={{0,30},{2,0},{4,2},{6,4},{8,6},{10,8},{12,10},{14,12},{16,14},{18,... | collective-permute-start | bytes 786440 | tf_op jit(solution)/shard_map/ppermute | solution.py:25
  273.7 4.6 %collective-permute-done.28 = bf16[16,2,4096]{2,0,1:T(8,128)(2,1)S(1)} collective-permute-done((bf16[16,2,4096]{2,0,1:T(8,128)(2,1)S(1)}, bf16[16,2,4096]{2,0,1:T(8,128)(2,1)S(1)}, u32[]{:S(2)}, u32[]{:S(2)}) %collective-permute-start.28) | collective-permute-done | bytes 262176 | tf_op jit(solution)/shard_map/ppermute | solution.py:20
  278.4 9.6 %collective-permute-done.30 = bf16[16,2,4096]{2,0,1:T(8,128)(2,1)S(1)} collective-permute-done((bf16[16,2,4096]{2,0,1:T(8,128)(2,1)S(1)}, bf16[16,2,4096]{2,0,1:T(8,128)(2,1)S(1)}, u32[]{:S(2)}, u32[]{:S(2)}) %collective-permute-start.30) | collective-permute-done | bytes 262176 | tf_op jit(solution)/shard_map/ppermute | solution.py:20
  297.9 5.1 %add_convert_fusion = bf16[256,2,4096]{2,0,1:T(8,128)(2,1)} fusion(bf16[256,2,768]{2,0,1:T(8,128)(2,1)S(1)} %multiply_convert_fusion, bf16[1,768,4096]{2,1,0:T(8,128)(2,1)S(1)} %bitcast.129, f32[256,2]{0,1:T(2,128)S(1)} %fusion.42, f32[2,4096]{1,0:T(2,128)S(1)} %bitcast_convert_fusion), kind=kOutput, calls=%fused_computation | convolution fusion | flops 3227516928 | bytes 11307008 | tf_op jit(solution)/shard_map/rkf,fd->rkd/dot_general | solution.py:76
  305.1 6.3 %all-reduce = s32[8]{0:T(128)S(1)} all-reduce(s32[8]{0:T(128)S(1)} %dynamic-update-slice), channel_id=1, replica_groups=mesh['pop'=4,'tp'=16,'pp'=2] {'pop'}, use_global_device_ids=true, to_apply=%add | all-reduce | flops 8 | bytes 64
  311.5 7.2 %all-gather = bf16[4,2,14592]{2,1,0:T(2,128)(2,1)S(1)} all-gather(bf16[1,2,14592]{2,1,0:T(2,128)(2,1)S(1)} %bitcast.113), channel_id=1, replica_groups=mesh['pop'=4,'tp'=16,'pp'=2] {'pop'}, dimensions={0}, use_global_device_ids=true | all-gather | bytes 291840 | tf_op jit(solution)/shard_map/all_gather | solution.py:40
  328.1 4.5 %fusion.52 = bf16[4,1024,768]{2,1,0:T(8,128)(2,1)} fusion(bf16[4,2,1024]{2,1,0:T(2,128)(2,1)S(1)} %reshape.58, bf16[4,2,768]{2,1,0:T(2,128)(2,1)S(1)} %reshape.59), kind=kOutput, calls=%fused_computation.111 | convolution fusion | flops 12582912 | bytes 6320128 | tf_op jit(solution)/shard_map/gmi,gmj->gij/dot_general | solution.py:90
  332.6 6.0 %reduce_sum.58 = bf16[768,1024]{1,0:T(8,128)(2,1)} reduce(bf16[4,768,1024]{2,1,0:T(8,128)(2,1)} %fusion.51, bf16[]{:T(256)} %constant.152.clone.1), dimensions={0}, to_apply=%region_6.7 | reduce | flops 2359296 | bytes 7864322 | tf_op jit(solution)/shard_map/reduce_sum | solution.py:92
  338.7 5.3 %reduce_sum.56 = bf16[1024,768]{1,0:T(8,128)(2,1)} reduce(bf16[4,1024,768]{2,1,0:T(8,128)(2,1)} %fusion.53, bf16[]{:T(256)} %constant.152.clone.1), dimensions={0}, to_apply=%region_4.5 | reduce | flops 2359296 | bytes 7864322 | tf_op jit(solution)/shard_map/reduce_sum | solution.py:92
  344.0 5.5 %reduce_sum.57 = bf16[1024,768]{1,0:T(8,128)(2,1)} reduce(bf16[4,1024,768]{2,1,0:T(8,128)(2,1)} %fusion.52, bf16[]{:T(256)} %constant.152.clone.1), dimensions={0}, to_apply=%region_5.6 | reduce | flops 2359296 | bytes 7864322 | tf_op jit(solution)/shard_map/reduce_sum | solution.py:92
  349.5 29.1 %reduce-scatter.5.cloned.1.call-done = bf16[16,2,4096]{2,0,1:T(8,128)(2,1)} async-done(((bf16[256,2,4096]{2,0,1:T(8,128)(2,1)}), bf16[16,2,4096]{2,0,1:T(8,128)(2,1)}) %reduce-scatter.5.cloned.1.call-update) | async-done | bytes 262160 | tf_op jit(solution)/shard_map/reduce_scatter | solution.py:78
  (174 shorter events, 96.3 us)
Async XLA Ops:
  7.2 186.9 %reduce-scatter.3.cloned.1.call-start = ((), (), s32[]{:S(2)}) async-start(), calls=%async_computation.2 | async-start | bytes 4456448 | tf_op jit(solution)/shard_map/reduce_scatter | solution.py:78
  12.1 12.6 %collective-permute-start = (bf16[16,2,4096]{2,0,1:T(8,128)(2,1)S(1)}, bf16[16,2,4096]{2,0,1:T(8,128)(2,1)S(1)}, u32[]{:S(2)}, u32[]{:S(2)}) collective-permute-start(bf16[16,2,4096]{2,0,1:T(8,128)(2,1)S(1)} %get-tuple-element.15), channel_id=1, source_target_pairs={{0,2},{2,4},{4,6},{6,8},{8,10},{10,12},{12,14},{14,16},{16,18},{18... | collective-permute-start | bytes 786440 | tf_op jit(solution)/shard_map/ppermute | solution.py:20
  13.7 11.0 %collective-permute-start.1 = (bf16[16,2,4096]{2,0,1:T(8,128)(2,1)S(1)}, bf16[16,2,4096]{2,0,1:T(8,128)(2,1)S(1)}, u32[]{:S(2)}, u32[]{:S(2)}) collective-permute-start(bf16[16,2,4096]{2,0,1:T(8,128)(2,1)S(1)} %get-tuple-element.15), channel_id=1, source_target_pairs={{0,30},{2,0},{4,2},{6,4},{8,6},{10,8},{12,10},{14,12},{16,14},{18,... | collective-permute-start | bytes 786440 | tf_op jit(solution)/shard_map/ppermute | solution.py:25
  24.7 10.8 %collective-permute-start.2 = (bf16[16,2,4096]{2,0,1:T(8,128)(2,1)S(1)}, bf16[16,2,4096]{2,0,1:T(8,128)(2,1)S(1)}, u32[]{:S(2)}, u32[]{:S(2)}) collective-permute-start(bf16[16,2,4096]{2,0,1:T(8,128)(2,1)S(1)} %collective-permute-done), channel_id=1, source_target_pairs={{0,2},{2,4},{4,6},{6,8},{8,10},{10,12},{12,14},{14,16},{16,18},{18... | collective-permute-start | bytes 786440 | tf_op jit(solution)/shard_map/ppermute | solution.py:20
  24.7 10.8 %collective-permute-start.3 = (bf16[16,2,4096]{2,0,1:T(8,128)(2,1)S(1)}, bf16[16,2,4096]{2,0,1:T(8,128)(2,1)S(1)}, u32[]{:S(2)}, u32[]{:S(2)}) collective-permute-start(bf16[16,2,4096]{2,0,1:T(8,128)(2,1)S(1)} %collective-permute-done.1), channel_id=1, source_target_pairs={{0,30},{2,0},{4,2},{6,4},{8,6},{10,8},{12,10},{14,12},{16,14},{18,... | collective-permute-start | bytes 786440 | tf_op jit(solution)/shard_map/ppermute | solution.py:25
  35.5 9.9 %collective-permute-start.4 = (bf16[16,2,4096]{2,0,1:T(8,128)(2,1)S(1)}, bf16[16,2,4096]{2,0,1:T(8,128)(2,1)S(1)}, u32[]{:S(2)}, u32[]{:S(2)}) collective-permute-start(bf16[16,2,4096]{2,0,1:T(8,128)(2,1)S(1)} %collective-permute-done.2), channel_id=1, source_target_pairs={{0,2},{2,4},{4,6},{6,8},{8,10},{10,12},{12,14},{14,16},{16,18},{18... | collective-permute-start | bytes 786440 | tf_op jit(solution)/shard_map/ppermute | solution.py:20
  35.5 9.9 %collective-permute-start.5 = (bf16[16,2,4096]{2,0,1:T(8,128)(2,1)S(1)}, bf16[16,2,4096]{2,0,1:T(8,128)(2,1)S(1)}, u32[]{:S(2)}, u32[]{:S(2)}) collective-permute-start(bf16[16,2,4096]{2,0,1:T(8,128)(2,1)S(1)} %collective-permute-done.3), channel_id=1, source_target_pairs={{0,30},{2,0},{4,2},{6,4},{8,6},{10,8},{12,10},{14,12},{16,14},{18,... | collective-permute-start | bytes 786440 | tf_op jit(solution)/shard_map/ppermute | solution.py:25
  45.4 9.7 %collective-permute-start.6 = (bf16[16,2,4096]{2,0,1:T(8,128)(2,1)S(1)}, bf16[16,2,4096]{2,0,1:T(8,128)(2,1)S(1)}, u32[]{:S(2)}, u32[]{:S(2)}) collective-permute-start(bf16[16,2,4096]{2,0,1:T(8,128)(2,1)S(1)} %collective-permute-done.4), channel_id=1, source_target_pairs={{0,2},{2,4},{4,6},{6,8},{8,10},{10,12},{12,14},{14,16},{16,18},{18... | collective-permute-start | bytes 786440 | tf_op jit(solution)/shard_map/ppermute | solution.py:20
  45.4 9.7 %collective-permute-start.7 = (bf16[16,2,4096]{2,0,1:T(8,128)(2,1)S(1)}, bf16[16,2,4096]{2,0,1:T(8,128)(2,1)S(1)}, u32[]{:S(2)}, u32[]{:S(2)}) collective-permute-start(bf16[16,2,4096]{2,0,1:T(8,128)(2,1)S(1)} %collective-permute-done.5), channel_id=1, source_target_pairs={{0,30},{2,0},{4,2},{6,4},{8,6},{10,8},{12,10},{14,12},{16,14},{18,... | collective-permute-start | bytes 786440 | tf_op jit(solution)/shard_map/ppermute | solution.py:25
  55.1 9.7 %collective-permute-start.8 = (bf16[16,2,4096]{2,0,1:T(8,128)(2,1)S(1)}, bf16[16,2,4096]{2,0,1:T(8,128)(2,1)S(1)}, u32[]{:S(2)}, u32[]{:S(2)}) collective-permute-start(bf16[16,2,4096]{2,0,1:T(8,128)(2,1)S(1)} %collective-permute-done.6), channel_id=1, source_target_pairs={{0,2},{2,4},{4,6},{6,8},{8,10},{10,12},{12,14},{14,16},{16,18},{18... | collective-permute-start | bytes 786440 | tf_op jit(solution)/shard_map/ppermute | solution.py:20
  55.1 9.7 %collective-permute-start.9 = (bf16[16,2,4096]{2,0,1:T(8,128)(2,1)S(1)}, bf16[16,2,4096]{2,0,1:T(8,128)(2,1)S(1)}, u32[]{:S(2)}, u32[]{:S(2)}) collective-permute-start(bf16[16,2,4096]{2,0,1:T(8,128)(2,1)S(1)} %collective-permute-done.7), channel_id=1, source_target_pairs={{0,30},{2,0},{4,2},{6,4},{8,6},{10,8},{12,10},{14,12},{16,14},{18,... | collective-permute-start | bytes 786440 | tf_op jit(solution)/shard_map/ppermute | solution.py:25
  64.8 9.7 %collective-permute-start.10 = (bf16[16,2,4096]{2,0,1:T(8,128)(2,1)S(1)}, bf16[16,2,4096]{2,0,1:T(8,128)(2,1)S(1)}, u32[]{:S(2)}, u32[]{:S(2)}) collective-permute-start(bf16[16,2,4096]{2,0,1:T(8,128)(2,1)S(1)} %collective-permute-done.8), channel_id=1, source_target_pairs={{0,2},{2,4},{4,6},{6,8},{8,10},{10,12},{12,14},{14,16},{16,18},{18... | collective-permute-start | bytes 786440 | tf_op jit(solution)/shard_map/ppermute | solution.py:20
  64.8 9.7 %collective-permute-start.11 = (bf16[16,2,4096]{2,0,1:T(8,128)(2,1)S(1)}, bf16[16,2,4096]{2,0,1:T(8,128)(2,1)S(1)}, u32[]{:S(2)}, u32[]{:S(2)}) collective-permute-start(bf16[16,2,4096]{2,0,1:T(8,128)(2,1)S(1)} %collective-permute-done.9), channel_id=1, source_target_pairs={{0,30},{2,0},{4,2},{6,4},{8,6},{10,8},{12,10},{14,12},{16,14},{18,... | collective-permute-start | bytes 786440 | tf_op jit(solution)/shard_map/ppermute | solution.py:25
  74.5 10.4 %collective-permute-start.12 = (bf16[16,2,4096]{2,0,1:T(8,128)(2,1)S(1)}, bf16[16,2,4096]{2,0,1:T(8,128)(2,1)S(1)}, u32[]{:S(2)}, u32[]{:S(2)}) collective-permute-start(bf16[16,2,4096]{2,0,1:T(8,128)(2,1)S(1)} %collective-permute-done.10), channel_id=1, source_target_pairs={{0,2},{2,4},{4,6},{6,8},{8,10},{10,12},{12,14},{14,16},{16,18},{18... | collective-permute-start | bytes 786440 | tf_op jit(solution)/shard_map/ppermute | solution.py:20
  74.5 11.5 %collective-permute-start.13 = (bf16[16,2,4096]{2,0,1:T(8,128)(2,1)S(1)}, bf16[16,2,4096]{2,0,1:T(8,128)(2,1)S(1)}, u32[]{:S(2)}, u32[]{:S(2)}) collective-permute-start(bf16[16,2,4096]{2,0,1:T(8,128)(2,1)S(1)} %collective-permute-done.11), channel_id=1, source_target_pairs={{0,30},{2,0},{4,2},{6,4},{8,6},{10,8},{12,10},{14,12},{16,14},{18,... | collective-permute-start | bytes 786440 | tf_op jit(solution)/shard_map/ppermute | solution.py:25
  84.9 10.1 %collective-permute-start.14 = (bf16[16,2,4096]{2,0,1:T(8,128)(2,1)S(1)}, bf16[16,2,4096]{2,0,1:T(8,128)(2,1)S(1)}, u32[]{:S(2)}, u32[]{:S(2)}) collective-permute-start(bf16[16,2,4096]{2,0,1:T(8,128)(2,1)S(1)} %collective-permute-done.12), channel_id=1, source_target_pairs={{0,2},{2,4},{4,6},{6,8},{8,10},{10,12},{12,14},{14,16},{16,18},{18... | collective-permute-start | bytes 786440 | tf_op jit(solution)/shard_map/ppermute | solution.py:20
  119.7 258.9 %reduce-scatter.5.cloned.1.call-start = ((), (), s32[]{:S(2)}) async-start(), calls=%async_computation.3 | async-start | bytes 4456448 | tf_op jit(solution)/shard_map/reduce_scatter | solution.py:78
  203.4 9.8 %collective-permute-start.16 = (bf16[16,2,4096]{2,0,1:T(8,128)(2,1)S(1)}, bf16[16,2,4096]{2,0,1:T(8,128)(2,1)S(1)}, u32[]{:S(2)}, u32[]{:S(2)}) collective-permute-start(bf16[16,2,4096]{2,0,1:T(8,128)(2,1)S(1)} %get-tuple-element.13), channel_id=1, source_target_pairs={{0,2},{2,4},{4,6},{6,8},{8,10},{10,12},{12,14},{14,16},{16,18},{18... | collective-permute-start | bytes 786440 | tf_op jit(solution)/shard_map/ppermute | solution.py:20
  204.7 8.5 %collective-permute-start.17 = (bf16[16,2,4096]{2,0,1:T(8,128)(2,1)S(1)}, bf16[16,2,4096]{2,0,1:T(8,128)(2,1)S(1)}, u32[]{:S(2)}, u32[]{:S(2)}) collective-permute-start(bf16[16,2,4096]{2,0,1:T(8,128)(2,1)S(1)} %get-tuple-element.13), channel_id=1, source_target_pairs={{0,30},{2,0},{4,2},{6,4},{8,6},{10,8},{12,10},{14,12},{16,14},{18,... | collective-permute-start | bytes 786440 | tf_op jit(solution)/shard_map/ppermute | solution.py:25
  213.1 9.7 %collective-permute-start.18 = (bf16[16,2,4096]{2,0,1:T(8,128)(2,1)S(1)}, bf16[16,2,4096]{2,0,1:T(8,128)(2,1)S(1)}, u32[]{:S(2)}, u32[]{:S(2)}) collective-permute-start(bf16[16,2,4096]{2,0,1:T(8,128)(2,1)S(1)} %collective-permute-done.16), channel_id=1, source_target_pairs={{0,2},{2,4},{4,6},{6,8},{8,10},{10,12},{12,14},{14,16},{16,18},{18... | collective-permute-start | bytes 786440 | tf_op jit(solution)/shard_map/ppermute | solution.py:20
  213.2 9.7 %collective-permute-start.19 = (bf16[16,2,4096]{2,0,1:T(8,128)(2,1)S(1)}, bf16[16,2,4096]{2,0,1:T(8,128)(2,1)S(1)}, u32[]{:S(2)}, u32[]{:S(2)}) collective-permute-start(bf16[16,2,4096]{2,0,1:T(8,128)(2,1)S(1)} %collective-permute-done.17), channel_id=1, source_target_pairs={{0,30},{2,0},{4,2},{6,4},{8,6},{10,8},{12,10},{14,12},{16,14},{18,... | collective-permute-start | bytes 786440 | tf_op jit(solution)/shard_map/ppermute | solution.py:25
  222.8 9.9 %collective-permute-start.20 = (bf16[16,2,4096]{2,0,1:T(8,128)(2,1)S(1)}, bf16[16,2,4096]{2,0,1:T(8,128)(2,1)S(1)}, u32[]{:S(2)}, u32[]{:S(2)}) collective-permute-start(bf16[16,2,4096]{2,0,1:T(8,128)(2,1)S(1)} %collective-permute-done.18), channel_id=1, source_target_pairs={{0,2},{2,4},{4,6},{6,8},{8,10},{10,12},{12,14},{14,16},{16,18},{18... | collective-permute-start | bytes 786440 | tf_op jit(solution)/shard_map/ppermute | solution.py:20
  222.9 9.8 %collective-permute-start.21 = (bf16[16,2,4096]{2,0,1:T(8,128)(2,1)S(1)}, bf16[16,2,4096]{2,0,1:T(8,128)(2,1)S(1)}, u32[]{:S(2)}, u32[]{:S(2)}) collective-permute-start(bf16[16,2,4096]{2,0,1:T(8,128)(2,1)S(1)} %collective-permute-done.19), channel_id=1, source_target_pairs={{0,30},{2,0},{4,2},{6,4},{8,6},{10,8},{12,10},{14,12},{16,14},{18,... | collective-permute-start | bytes 786440 | tf_op jit(solution)/shard_map/ppermute | solution.py:25
  232.7 10.8 %collective-permute-start.22 = (bf16[16,2,4096]{2,0,1:T(8,128)(2,1)S(1)}, bf16[16,2,4096]{2,0,1:T(8,128)(2,1)S(1)}, u32[]{:S(2)}, u32[]{:S(2)}) collective-permute-start(bf16[16,2,4096]{2,0,1:T(8,128)(2,1)S(1)} %collective-permute-done.20), channel_id=1, source_target_pairs={{0,2},{2,4},{4,6},{6,8},{8,10},{10,12},{12,14},{14,16},{16,18},{18... | collective-permute-start | bytes 786440 | tf_op jit(solution)/shard_map/ppermute | solution.py:20
  232.7 11.1 %collective-permute-start.23 = (bf16[16,2,4096]{2,0,1:T(8,128)(2,1)S(1)}, bf16[16,2,4096]{2,0,1:T(8,128)(2,1)S(1)}, u32[]{:S(2)}, u32[]{:S(2)}) collective-permute-start(bf16[16,2,4096]{2,0,1:T(8,128)(2,1)S(1)} %collective-permute-done.21), channel_id=1, source_target_pairs={{0,30},{2,0},{4,2},{6,4},{8,6},{10,8},{12,10},{14,12},{16,14},{18,... | collective-permute-start | bytes 786440 | tf_op jit(solution)/shard_map/ppermute | solution.py:25
  243.5 12.3 %collective-permute-start.24 = (bf16[16,2,4096]{2,0,1:T(8,128)(2,1)S(1)}, bf16[16,2,4096]{2,0,1:T(8,128)(2,1)S(1)}, u32[]{:S(2)}, u32[]{:S(2)}) collective-permute-start(bf16[16,2,4096]{2,0,1:T(8,128)(2,1)S(1)} %collective-permute-done.22), channel_id=1, source_target_pairs={{0,2},{2,4},{4,6},{6,8},{8,10},{10,12},{12,14},{14,16},{16,18},{18... | collective-permute-start | bytes 786440 | tf_op jit(solution)/shard_map/ppermute | solution.py:20
  243.9 12.4 %collective-permute-start.25 = (bf16[16,2,4096]{2,0,1:T(8,128)(2,1)S(1)}, bf16[16,2,4096]{2,0,1:T(8,128)(2,1)S(1)}, u32[]{:S(2)}, u32[]{:S(2)}) collective-permute-start(bf16[16,2,4096]{2,0,1:T(8,128)(2,1)S(1)} %collective-permute-done.23), channel_id=1, source_target_pairs={{0,30},{2,0},{4,2},{6,4},{8,6},{10,8},{12,10},{14,12},{16,14},{18,... | collective-permute-start | bytes 786440 | tf_op jit(solution)/shard_map/ppermute | solution.py:25
  255.8 11.7 %collective-permute-start.26 = (bf16[16,2,4096]{2,0,1:T(8,128)(2,1)S(1)}, bf16[16,2,4096]{2,0,1:T(8,128)(2,1)S(1)}, u32[]{:S(2)}, u32[]{:S(2)}) collective-permute-start(bf16[16,2,4096]{2,0,1:T(8,128)(2,1)S(1)} %collective-permute-done.24), channel_id=1, source_target_pairs={{0,2},{2,4},{4,6},{6,8},{8,10},{10,12},{12,14},{14,16},{16,18},{18... | collective-permute-start | bytes 786440 | tf_op jit(solution)/shard_map/ppermute | solution.py:20
  256.3 11.6 %collective-permute-start.27 = (bf16[16,2,4096]{2,0,1:T(8,128)(2,1)S(1)}, bf16[16,2,4096]{2,0,1:T(8,128)(2,1)S(1)}, u32[]{:S(2)}, u32[]{:S(2)}) collective-permute-start(bf16[16,2,4096]{2,0,1:T(8,128)(2,1)S(1)} %collective-permute-done.25), channel_id=1, source_target_pairs={{0,30},{2,0},{4,2},{6,4},{8,6},{10,8},{12,10},{14,12},{16,14},{18,... | collective-permute-start | bytes 786440 | tf_op jit(solution)/shard_map/ppermute | solution.py:25
  267.5 10.9 %collective-permute-start.28 = (bf16[16,2,4096]{2,0,1:T(8,128)(2,1)S(1)}, bf16[16,2,4096]{2,0,1:T(8,128)(2,1)S(1)}, u32[]{:S(2)}, u32[]{:S(2)}) collective-permute-start(bf16[16,2,4096]{2,0,1:T(8,128)(2,1)S(1)} %collective-permute-done.26), channel_id=1, source_target_pairs={{0,2},{2,4},{4,6},{6,8},{8,10},{10,12},{12,14},{14,16},{16,18},{18... | collective-permute-start | bytes 786440 | tf_op jit(solution)/shard_map/ppermute | solution.py:20
  267.9 10.5 %collective-permute-start.29 = (bf16[16,2,4096]{2,0,1:T(8,128)(2,1)S(1)}, bf16[16,2,4096]{2,0,1:T(8,128)(2,1)S(1)}, u32[]{:S(2)}, u32[]{:S(2)}) collective-permute-start(bf16[16,2,4096]{2,0,1:T(8,128)(2,1)S(1)} %collective-permute-done.27), channel_id=1, source_target_pairs={{0,30},{2,0},{4,2},{6,4},{8,6},{10,8},{12,10},{14,12},{16,14},{18,... | collective-permute-start | bytes 786440 | tf_op jit(solution)/shard_map/ppermute | solution.py:25
  278.3 9.7 %collective-permute-start.30 = (bf16[16,2,4096]{2,0,1:T(8,128)(2,1)S(1)}, bf16[16,2,4096]{2,0,1:T(8,128)(2,1)S(1)}, u32[]{:S(2)}, u32[]{:S(2)}) collective-permute-start(bf16[16,2,4096]{2,0,1:T(8,128)(2,1)S(1)} %collective-permute-done.28), channel_id=1, source_target_pairs={{0,2},{2,4},{4,6},{6,8},{8,10},{10,12},{12,14},{14,16},{16,18},{18... | collective-permute-start | bytes 786440 | tf_op jit(solution)/shard_map/ppermute | solution.py:20
  (23 other events, 301.5 us)
Sparse Core Ops, SparseCore 0:
  119.8 74.2 reduce-scatter.2
  303.1 75.4 reduce-scatter.4
